TPU v7x, 32 devices: a whole 2x2x4 slice. The times are simulated.
32 devices in a mesh: gx: 4 (over z), gy: 8 (over y, x, core).
Axes of the slice: x: 2, y: 2, z: 4, core: 2. Of those that a mesh axis runs over, the one named last changes fastest.
Arguments:
- wavefield: float32 [9, 56, 4096], P(None, None, ('gx', 'gy')), may hold values from -6 to 6
- star_mats: float32 [3, 9, 9, 4096], P(None, None, None, ('gx', 'gy')), may hold values from -1 to 1
- flux_own: float32 [4, 9, 9, 4096], P(None, None, None, ('gx', 'gy')), may hold values from -0.8 to 0.8
- flux_nbr: float32 [4, 9, 9, 4096], P(None, None, None, ('gx', 'gy')), may hold values from -0.8 to 0.8
- stiffness: float32 [3, 56, 56], replicated, may hold values from -0.75 to 0.75
- face_proj: float32 [4, 21, 56], replicated, may hold values from -0.75 to 0.75
- lift_mats: float32 [4, 56, 21], replicated, may hold values from -1.25 to 1.25
- cluster: int32 [4096], P(('gx', 'gy')), may hold values from 0 to 1
- yield_stress: float32 [4096], P(('gx', 'gy')), may hold values from 0.5 to 5
- plastic_mask: int32 [4096], P(('gx', 'gy')), may hold values from 0 to 1
- face_source: int32 [4, 4096], P(None, ('gx', 'gy')), may hold values from 0 to 639, as said below
- send_faces: int32 [128, 32], P(('gx', 'gy')), may hold values from 0 to 511, as said below
- fault_faces: int32 [32, 64], P(('gx', 'gy')), may hold values from 0 to 511, as said below
- fault_owner: int32 [2048, 1], P(('gx', 'gy')), may hold values from 0 to 7; in each aligned block of 64 rows (0 to 63, 64 to 127, ...) at most 16 rows name the same one
- fault_slip: float32 [4096], P(('gx', 'gy')), may hold values from 0 to 1
- cohesion: float32 [4096], P(('gx', 'gy')), may hold values from 0.1 to 1
- slip_flag: int32 [4096], P(('gx', 'gy')), may hold values from 0 to 1
Outputs:
- wavefield_out: float32 [9, 56, 4096], P(None, None, ('gx', 'gy'))
- slip_out: float32 [4096], P(('gx', 'gy'))
Inputs may be any that keep to these rules, and one draw needn't show every extreme that they name: `face_source`: entries below 512 name the partition's own faces; every received slot is named by exactly one face of its partition. `send_faces`: entries of one row are distinct. `fault_faces`: entries of one partition are distinct. `fault_owner`: among the fault faces of one partition at most 16 name the same owner.
All inputs are finite; a program needn't handle non-finite values.
Results may differ from a plain program's by a relative error of at most 0.0001.
Values sent between devices are 32-bit elements; how exact they have to be, the bound alone decides.
A program may use at most 64 MiB of HBM per device.

v0:
```python
import functools
import math

import jax
import jax.numpy as jnp
from jax import lax
from jax.experimental import pallas as pl
from jax.experimental.pallas import tpu as pltpu
from jax.sharding import PartitionSpec as P

VARS = 9
ORDER = 6
HIGHEST = lax.Precision.HIGHEST
F32 = jnp.float32
BF16 = jnp.bfloat16


def up8(n):
    return -(-n // 8) * 8


def iota_f(shape, axis):
    return lax.broadcasted_iota(jnp.int32, shape, axis).astype(F32)


def dot(a, b):
    return jnp.dot(a, b, preferred_element_type=F32)


def low_part(x):
    return x - x.astype(BF16).astype(F32)


def two_parts(x):
    return jnp.concatenate([x, low_part(x)], axis=0).astype(BF16)


def dot_split(mat, data):
    rows = mat.shape[0]
    top = dot(two_parts(mat), data.astype(BF16))
    return top[:rows] + (top[rows:] + dot(mat.astype(BF16), low_part(data).astype(BF16)))


def pick(parts, select):
    rows = parts.shape[0] // 2
    both = dot(parts, select)
    return both[:rows] + both[rows:]


def kernel(
    cfg,
    wave,
    star,
    own_mats,
    nbr_mats,
    stiff,
    stiff_t,
    proj,
    lift,
    cluster,
    yield_stress,
    mask,
    source,
    sends,
    faults,
    owners,
    slip0,
    cohesion,
    flag,
    out,
    slip_out,
    deriv,
    early,
    late,
    mid,
    inc,
    carried,
    mix,
    own_tab,
    nbr_tab,
    flux,
    select,
    send_select,
    fault_select,
    slots,
    par,
    face_par,
    moved,
    ret,
    got,
    packs,
    recs,
    table_in,
    par_send,
    par_recv,
    ret_send,
    ret_recv,
    tr_send,
    tr_recv,
):
    nx, ny, points = cfg
    modes, elems = wave.shape[1:]
    rows = up8(points)
    faces = 4 * elems
    slot_count = sends.shape[1] // 4
    group = packs.shape[2]
    table_rows = VARS * rows
    cap = slip0.shape[1] // ny
    ix, iy = lax.axis_index("gx"), lax.axis_index("gy")
    x_up = (lax.rem(ix + 1, nx), iy)
    x_down = (lax.rem(ix + nx - 1, nx), iy)
    y_up = (ix, lax.rem(iy + 1, ny))
    y_down = (ix, lax.rem(iy + ny - 1, ny))
    MESH = pl.DeviceIdType.MESH

    def peer(step):
        return (ix, lax.rem(iy + step, ny))

    barrier = pltpu.get_barrier_semaphore()
    for target in [x_up, x_down] + [peer(t) for t in range(1, ny)]:
        pl.semaphore_signal(barrier, inc=1, device_id=target, device_id_type=MESH)

    me = iy.astype(F32)
    table_size = select.shape[0]
    for f in range(4):
        want = source[f : f + 1, :].astype(F32)
        hit = iota_f((table_size, elems), 0) == want
        select[:, f * elems : (f + 1) * elems] = jnp.where(hit, 1.0, 0.0).astype(BF16)
    hit = iota_f((faces, 4 * slot_count), 0) == sends[...].astype(F32)
    send_select[...] = jnp.where(hit, 1.0, 0.0).astype(BF16)
    count = faults.shape[1]
    hit = iota_f((faces, count), 0) == faults[...].astype(F32)
    fault_select[...] = jnp.where(hit, 1.0, 0.0)
    owner_col = owners[...].astype(F32)
    r, c = iota_f((count, count), 0), iota_f((count, count), 1)
    owner_row = jnp.sum(jnp.where(r == c, owner_col, 0.0), axis=0, keepdims=True)
    same = jnp.where((owner_col == owner_row) & (r < c), 1.0, 0.0)
    rank = jnp.sum(same, axis=0, keepdims=True)
    slot_row = me * cap + rank
    slots[...] = jnp.where(iota_f((slip0.shape[1], count), 0) == slot_row, 1.0, 0.0)
    away = owner_row - me
    ahead = jnp.where(away < 0, away + ny, away)
    behind = jnp.where(away > 0, ny - away, -away)

    def mix_all(src, field):
        def one_dir(d, carry):
            at = pl.ds(pl.multiple_of(d * modes, 8), modes)
            for first in range(0, VARS, 3):
                accs = [None] * 3
                for s in range(VARS):
                    value = field[s]
                    for k in range(3):
                        term = star[d, first + k, s : s + 1, :] * value
                        accs[k] = term if s == 0 else accs[k] + term
                for k in range(3):
                    mix[at, (first + k) * elems : (first + k + 1) * elems] = accs[k]
            return carry

        lax.fori_loop(0, 3, one_dir, 0)

    def predict(src, with_late):
        for v in range(VARS):
            deriv[v] = src[v]
            early[v] = src[v]
            if with_late:
                late[v] = src[v]

        def one_power(power, carry):
            scale_early = jnp.float32(0.0)
            scale_late = jnp.float32(0.0)
            for p in range(2, ORDER + 1):
                scale_early = jnp.where(power == p, 1.0 / math.factorial(p), scale_early)
                scale_late = jnp.where(
                    power == p, (2.0**p - 1.0) / math.factorial(p), scale_late
                )
            mix_all(None, deriv)
            change = dot_split(stiff[...], mix[...])
            for v in range(VARS):
                step = -change[:, v * elems : (v + 1) * elems]
                deriv[v] = step
                early[v] += step * scale_early
                if with_late:
                    late[v] += step * scale_late
            return carry

        lax.fori_loop(2, ORDER + 1, one_power, 0)

    def advance(field, turn):
        flat = jnp.concatenate([field[v] for v in range(VARS)], axis=1)
        traces = dot_split(proj[...], flat)
        for v in range(VARS):
            for f in range(4):
                own_tab[v * rows : (v + 1) * rows, f * elems : (f + 1) * elems] = traces[
                    f * rows : (f + 1) * rows, v * elems : (v + 1) * elems
                ]
        own_parts = two_parts(own_tab[...])
        table_in[table_rows:, :] = jnp.zeros((4 * group - table_rows, 4 * slot_count), F32)
        table_in[0:table_rows, :] = pick(own_parts, send_select[...])
        lane_group = lax.broadcasted_iota(jnp.int32, (group, 4 * slot_count), 1) // slot_count
        copies = []
        for q, target in enumerate([x_up, x_down, y_up, y_down]):
            packed = jnp.zeros((group, 4 * slot_count), F32)
            for g in range(4):
                piece = table_in[g * group : (g + 1) * group, :]
                shift = ((g - q) % 4) * slot_count
                if shift:
                    piece = pltpu.roll(piece, shift, 1)
                packed = jnp.where(lane_group == g, piece, packed)
            packs[turn, q] = packed
            copy = pltpu.make_async_remote_copy(
                src_ref=packs.at[turn, q],
                dst_ref=recs.at[turn, q],
                send_sem=tr_send.at[turn, q],
                recv_sem=tr_recv.at[turn, q],
                device_id=target,
                device_id_type=MESH,
            )
            copy.start()
            copies.append(copy)

        mix_all(None, field)
        volume = dot_split(stiff_t[...], mix[...])
        for v in range(VARS):
            inc[v] = volume[:, v * elems : (v + 1) * elems]
        nbr_tab[...] = pick(own_parts, select[0:faces, :])

        def own_flux(f, carry):
            lanes = pl.ds(pl.multiple_of(f * elems, elems), elems)
            at = pl.ds(pl.multiple_of(f * rows, 8), rows)
            accs = [None] * VARS
            for s in range(VARS):
                value = own_tab[s * rows : (s + 1) * rows, lanes]
                for i in range(VARS):
                    term = own_mats[f, i, s : s + 1, :] * value
                    accs[i] = term if s == 0 else accs[i] + term
            for i in range(VARS):
                flux[at, i * elems : (i + 1) * elems] = accs[i]
            return carry

        lax.fori_loop(0, 4, own_flux, 0)
        if turn == 0:
            for copy in par_copies:
                copy.wait_recv()
            chosen = jnp.dot(
                par[...].reshape(ny * 8, par.shape[2]),
                slots[...],
                precision=HIGHEST,
                preferred_element_type=F32,
            )
            mine = jnp.zeros((8, count), F32)
            for t in range(ny):
                mine = jnp.where(behind == t, chosen[t * 8 : (t + 1) * 8], mine)
            face_par[...] = lax.dot_general(
                mine,
                fault_select[...],
                (((1,), (1,)), ((), ())),
                precision=HIGHEST,
                preferred_element_type=F32,
            )
            moved[...] = jnp.zeros_like(moved)
        for copy in copies:
            copy.wait_recv()
        for g in range(4):
            total = jnp.zeros((group, 4 * slot_count), F32)
            for q in range(4):
                piece = recs[turn, q]
                shift = ((q - g) % 4) * slot_count
                if shift:
                    piece = pltpu.roll(piece, shift, 1)
                total = jnp.where(lane_group == q, piece, total)
            table_in[g * group : (g + 1) * group, :] = total
        nbr_tab[...] += pick(two_parts(table_in[0:table_rows, :]), select[faces:, :])

        def face_flux(f, carry):
            lanes = pl.ds(pl.multiple_of(f * elems, elems), elems)
            at = pl.ds(pl.multiple_of(f * rows, 8), rows)
            accs = [None] * VARS
            for s in range(VARS):
                value = nbr_tab[s * rows : (s + 1) * rows, lanes]
                for i in range(VARS):
                    term = nbr_mats[f, i, s : s + 1, :] * value
                    accs[i] = term if s == 0 else accs[i] + term
            state = []
            for tv, vv in ((0, 6), (3, 7), (5, 8)):
                m_t = own_tab[tv * rows : (tv + 1) * rows, lanes]
                n_t = nbr_tab[tv * rows : (tv + 1) * rows, lanes]
                m_v = own_tab[vv * rows : (vv + 1) * rows, lanes]
                n_v = nbr_tab[vv * rows : (vv + 1) * rows, lanes]
                state.append(0.5 * (m_t + n_t) + 0.5 * (n_v - m_v))
            slip = face_par[0:1, lanes]
            coeff = 0.6 - 0.3 * jnp.minimum(slip / 0.5, 1.0)
            strength = face_par[1:2, lanes] + coeff * jnp.maximum(-state[0], 0.0)
            size = jnp.sqrt(state[1] * state[1] + state[2] * state[2])
            slipping = face_par[2:3, lanes] > 0.5
            ratio = jnp.where(slipping, strength / jnp.maximum(size, strength), 1.0)
            accs[3] = accs[3] + state[1] * (ratio - 1.0)
            accs[5] = accs[5] + state[2] * (ratio - 1.0)
            for i in range(VARS):
                flux[at, i * elems : (i + 1) * elems] += accs[i]
            gain = jnp.sum(size * (1.0 - ratio), axis=0, keepdims=True) / points
            face_par[0:1, lanes] = slip + gain
            moved[0:1, lanes] += gain
            return carry

        lax.fori_loop(0, 4, face_flux, 0)
        if turn == 1:
            per_fault = jnp.dot(
                moved[...], fault_select[...], precision=HIGHEST, preferred_element_type=F32
            )[0:1]
            ways = -(-ny // 8) * 8
            spread = jnp.where(iota_f((ways, count), 0) == ahead, per_fault, 0.0)
            to_slots = lax.dot_general(
                spread,
                slots[...],
                (((1,), (1,)), ((), ())),
                precision=HIGHEST,
                preferred_element_type=F32,
            )
            for t in range(ny):
                ret[t] = jnp.broadcast_to(to_slots[t : t + 1], ret.shape[1:])
            for t in range(1, ny):
                copy = pltpu.make_async_remote_copy(
                    src_ref=ret.at[t],
                    dst_ref=got.at[t],
                    send_sem=ret_send.at[t],
                    recv_sem=ret_recv.at[t],
                    device_id=peer(t),
                    device_id_type=MESH,
                )
                copy.start()
                ret_copies.append(copy)
        lifted = dot_split(lift[...], flux[...])
        for v in range(VARS):
            inc[v] -= lifted[:, v * elems : (v + 1) * elems]
        trace_copies.extend(copies)

    def plastic(values):
        mean = (values[0] + values[1] + values[2]) / 3.0
        dev = [values[v] - mean for v in range(3)]
        total = dev[0] * dev[0] + dev[1] * dev[1] + dev[2] * dev[2]
        shear = values[3] * values[3] + values[4] * values[4] + values[5] * values[5]
        second = jnp.sum(total + 2.0 * shear, axis=0, keepdims=True) / (2.0 * modes)
        equiv = jnp.sqrt(second + 1e-06)
        factor = 1.0 - mask[...].astype(F32) * 0.5 * jnp.maximum(
            1.0 - yield_stress[...] / equiv, 0.0
        )
        return [mean + factor * d for d in dev] + [factor * values[v] for v in range(3, 6)]

    par_copies, ret_copies, trace_copies = [], [], []
    predict(wave, True)
    pl.semaphore_wait(barrier, ny + 1)
    par[0] = jnp.zeros(par.shape[1:], F32)
    par[0, 0:1] = slip0[...]
    par[0, 1:2] = cohesion[...]
    par[0, 2:3] = flag[...].astype(F32)
    for t in range(1, ny):
        copy = pltpu.make_async_remote_copy(
            src_ref=par.at[0],
            dst_ref=par.at[t],
            send_sem=par_send.at[t],
            recv_sem=par_recv.at[t],
            device_id=peer(t),
            device_id_type=MESH,
        )
        copy.start()
        par_copies.append(copy)
    advance(early, 0)
    coarse = cluster[...] == 1
    tried = plastic([wave[v] + inc[v] for v in range(6)])
    for v in range(VARS):
        new = tried[v] if v < 6 else wave[v] + inc[v]
        carried[v] = jnp.where(coarse, inc[v], 0.0)
        mid[v] = jnp.where(coarse, wave[v], new)
    predict(mid, False)
    for v in range(VARS):
        early[v] = jnp.where(coarse, late[v], early[v])
    advance(early, 1)
    done = plastic([(mid[v] + inc[v]) + carried[v] for v in range(6)])
    for v in range(VARS):
        out[v] = done[v] if v < 6 else (mid[v] + inc[v]) + carried[v]
    total = slip0[...] + ret[0, 0:1]
    for t in range(1, ny):
        ret_copies[t - 1].wait_recv()
        total = total + got[t, 0:1]
    slip_out[...] = total
    for copy in par_copies + trace_copies + ret_copies:
        copy.wait_send()


def local(
    nx,
    ny,
    wavefield,
    star_mats,
    flux_own,
    flux_nbr,
    stiffness,
    face_proj,
    lift_mats,
    cluster,
    yield_stress,
    plastic_mask,
    face_source,
    send_faces,
    fault_faces,
    fault_owner,
    fault_slip,
    cohesion,
    slip_flag,
):
    modes, elems = wavefield.shape[1:]
    points = face_proj.shape[1]
    rows = up8(points)
    slot_count = send_faces.shape[1]
    count = fault_faces.shape[1]
    owned = fault_slip.shape[0]
    pad = rows - points
    stiff = jnp.transpose(stiffness, (1, 0, 2)).reshape(modes, 3 * modes)
    stiff_t = jnp.transpose(stiffness, (2, 0, 1)).reshape(modes, 3 * modes)
    proj = jnp.pad(face_proj, ((0, 0), (0, pad), (0, 0))).reshape(4 * rows, modes)
    lift = jnp.pad(jnp.transpose(lift_mats, (1, 0, 2)), ((0, 0), (0, 0), (0, pad)))
    lift = lift.reshape(modes, 4 * rows)
    sends = send_faces[jnp.array([1, 0, 3, 2])].reshape(1, 4 * slot_count)
    group = up8(-(-VARS * rows // 4))
    field = pltpu.VMEM((VARS, modes, elems), F32)
    vmem = pl.BlockSpec(memory_space=pltpu.VMEM)
    out, slip = pl.pallas_call(
        functools.partial(kernel, (nx, ny, points)),
        out_shape=(
            jax.ShapeDtypeStruct(wavefield.shape, F32),
            jax.ShapeDtypeStruct((1, owned), F32),
        ),
        in_specs=[vmem] * 18,
        out_specs=(vmem, vmem),
        scratch_shapes=[field] * 6
        + [
            pltpu.VMEM((3 * modes, VARS * elems), F32),
            pltpu.VMEM((VARS * rows, 4 * elems), F32),
            pltpu.VMEM((VARS * rows, 4 * elems), F32),
            pltpu.VMEM((4 * rows, VARS * elems), F32),
            pltpu.VMEM((4 * elems + 4 * slot_count, 4 * elems), BF16),
            pltpu.VMEM((4 * elems, 4 * slot_count), BF16),
            pltpu.VMEM((4 * elems, count), F32),
            pltpu.VMEM((owned, count), F32),
            pltpu.VMEM((ny, 8, owned), F32),
            pltpu.VMEM((8, 4 * elems), F32),
            pltpu.VMEM((8, 4 * elems), F32),
            pltpu.VMEM((ny, 8, owned), F32),
            pltpu.VMEM((ny, 8, owned), F32),
            pltpu.VMEM((2, 4, group, 4 * slot_count), F32),
            pltpu.VMEM((2, 4, group, 4 * slot_count), F32),
            pltpu.VMEM((4 * group, 4 * slot_count), F32),
            pltpu.SemaphoreType.DMA((ny,)),
            pltpu.SemaphoreType.DMA((ny,)),
            pltpu.SemaphoreType.DMA((ny,)),
            pltpu.SemaphoreType.DMA((ny,)),
            pltpu.SemaphoreType.DMA((2, 4)),
            pltpu.SemaphoreType.DMA((2, 4)),
        ],
        compiler_params=pltpu.CompilerParams(
            collective_id=0, has_side_effects=True, vmem_limit_bytes=48 * 1024 * 1024
        ),
    )(
        wavefield,
        star_mats,
        flux_own,
        flux_nbr,
        stiff,
        stiff_t,
        proj,
        lift,
        cluster.reshape(1, elems),
        yield_stress.reshape(1, elems),
        plastic_mask.reshape(1, elems),
        face_source,
        sends,
        fault_faces,
        fault_owner,
        fault_slip.reshape(1, owned),
        cohesion.reshape(1, owned),
        slip_flag.reshape(1, owned),
    )
    return (out, slip.reshape(owned))


def solution(mesh):
    both = ("gx", "gy")
    return jax.shard_map(
        functools.partial(local, mesh.shape["gx"], mesh.shape["gy"]),
        mesh=mesh,
        in_specs=(
            P(None, None, both),
            P(None, None, None, both),
            P(None, None, None, both),
            P(None, None, None, both),
            P(),
            P(),
            P(),
            P(both),
            P(both),
            P(both),
            P(None, both),
            P(both, None),
            P(both, None),
            P(both, None),
            P(both),
            P(both),
            P(both),
        ),
        out_specs=(P(None, None, both), P(both)),
        check_vma=False,
    )
```

profile of v0, /device:TPU:0, one launch (start us, length us, event | category | flops | bytes accessed | tf_op | source)
XLA Modules:
  0.0 35.4 jit_solution(11684931213821037588)
XLA Ops:
  0.6 0.0 copy-start
  0.6 0.0 copy-start.17
  0.7 0.0 copy-start.14
  0.7 0.6 %copy-done.17 = s32[4]{0:T(128)S(1)} copy-done((s32[4]{0:T(128)S(1)}, s32[4]{0:T(128)}, u32[]{:S(2)}) %copy-start.17) | copy-done | bytes 40
  1.3 0.0 copy-done
  1.3 0.6 %gather_fusion = s32[4,32]{1,0:T(4,128)S(1)} fusion(s32[4,32]{1,0:T(4,128)S(1)} %copy-done, s32[1024]{0:T(1024)S(1)} %pad_clamp_fusion), kind=kCustom, calls=%fused_computation | custom fusion | bytes 1040 | tf_op jit(solution)/shard_map/gather | solution.py:423
  1.9 0.0 copy-start.16
  1.9 0.1 reshape.47.sends
  2.0 0.6 %copy-done.16 = s32[64,1]{0,1:T(1,128)S(1)} copy-done((s32[64,1]{0,1:T(1,128)S(1)}, s32[64,1]{0,1:T(1,128)}, u32[]{:S(2)}) %copy-start.16) | copy-done | bytes 280
  2.5 0.1 copy.37.owners
  2.6 0.0 copy-done.14
  2.6 0.0 copy-start.15
  2.7 0.8 %copy-done.15 = f32[4,56,21]{1,0,2:T(4,128)S(1)} copy-done((f32[4,56,21]{1,0,2:T(4,128)S(1)}, f32[4,56,21]{1,0,2:T(4,128)}, u32[]{:S(2)}) %copy-start.15) | copy-done | bytes 18840
  3.4 0.0 copy-start.10
  3.5 0.1 copy.36.lift
  3.5 0.8 %copy-done.10 = f32[3,56,56]{2,1,0:T(8,128)S(1)} copy-done((f32[3,56,56]{2,1,0:T(8,128)S(1)}, f32[3,56,56]{2,1,0:T(8,128)}, u32[]{:S(2)}) %copy-start.10) | copy-done | bytes 37656
  4.3 0.1 copy.35.stiff_t
  4.4 0.0 copy-start.13
  4.4 0.1 copy.28
  4.5 0.1 copy.34.stiff
  4.6 0.7 %copy-done.13 = f32[3,9,9,128]{3,0,2,1:T(4,128)S(1)} copy-done((f32[3,9,9,128]{3,0,2,1:T(4,128)S(1)}, f32[3,9,9,128]{3,0,2,1:T(4,128)}, u32[]{:S(2)}) %copy-start.13) | copy-done | bytes 124440
  5.3 0.0 copy-start.11
  5.4 0.9 %copy-done.11 = f32[4,9,9,128]{3,0,2,1:T(4,128)S(1)} copy-done((f32[4,9,9,128]{3,0,2,1:T(4,128)S(1)}, f32[4,9,9,128]{3,0,2,1:T(4,128)}, u32[]{:S(2)}) %copy-start.11) | copy-done | bytes 165912
  6.2 0.0 copy-start.12
  6.3 0.9 %copy-done.12 = f32[4,9,9,128]{3,0,2,1:T(4,128)S(1)} copy-done((f32[4,9,9,128]{3,0,2,1:T(4,128)S(1)}, f32[4,9,9,128]{3,0,2,1:T(4,128)}, u32[]{:S(2)}) %copy-start.12) | copy-done | bytes 165912
  7.2 0.0 copy-start.1
  7.2 0.0 copy-start.2
  7.2 0.0 copy-start.3
  7.2 0.0 copy-start.4
  7.2 0.0 copy-start.5
  7.2 0.0 copy-start.6
  7.2 0.0 copy-start.7
  7.2 0.0 copy-start.8
  7.2 0.0 copy-start.9
  7.3 0.8 %copy-done.1 = f32[9,56,128]{2,1,0:T(8,128)S(1)} copy-done((f32[9,56,128]{2,1,0:T(8,128)S(1)}, f32[9,56,128]{2,1,0:T(8,128)}, u32[]{:S(2)}) %copy-start.1) | copy-done | bytes 258072
  8.1 0.0 copy-done.2
  8.1 0.0 copy-done.3
  8.1 0.0 copy-done.4
  8.1 0.0 copy-done.5
  8.1 0.0 copy-done.6
  8.1 0.0 copy-done.7
  8.1 0.0 copy-done.8
  8.2 0.0 copy-done.9
  8.2 26.0 %shard_map.185 = (f32[9,56,128]{2,1,0:T(8,128)S(1)}, f32[1,128]{1,0:T(1,128)S(1)}) custom-call(f32[9,56,128]{2,1,0:T(8,128)S(1)} %copy-done.1, f32[3,9,9,128]{3,2,1,0:T(8,128)S(1)} %copy.31.star, f32[4,9,9,128]{3,2,1,0:T(8,128)S(1)} %copy.32.own_mats, f32[4,9,9,128]{3,2,1,0:T(8,128)S(1)} %copy.33.nbr_mats, f32[56,168]{1,0:T(8,128)S(1)} %copy.34.stiff, ...), custom_call_target="tpu_custom_call" | custom-call | tf_op jit(solution)/shard_map/pallas_call | solution.py:427
  34.2 0.7 %copy.42 = f32[9,56,128]{2,1,0:T(8,128)} copy(f32[9,56,128]{2,1,0:T(8,128)S(1)} %get-tuple-element.8) | data formatting | bytes 516096
  34.9 0.5 %copy.43 = f32[128]{0:T(128)} copy(f32[128]{0:T(128)S(1)} %bitcast.22) | data formatting | bytes 1024
  (8 shorter events, 0.1 us)
Async XLA Ops:
  0.6 0.7 %copy-start = (s32[4,32]{1,0:T(4,128)S(1)}, s32[4,32]{1,0:T(4,128)}, u32[]{:S(2)}) copy-start(s32[4,32]{1,0:T(4,128)} %param.29) | copy-start | bytes 1540
  0.6 0.7 %copy-start.17 = (s32[4]{0:T(128)S(1)}, s32[4]{0:T(128)}, u32[]{:S(2)}) copy-start(s32[4]{0:T(128)} %constant.20) | copy-start | bytes 52
  0.7 2.0 %copy-start.14 = (f32[4,21,56]{2,0,1:T(4,128)S(1)}, f32[4,21,56]{2,0,1:T(4,128)}, u32[]{:S(2)}) copy-start(f32[4,21,56]{2,0,1:T(4,128)} %param.23) | copy-start | bytes 56452
  1.9 0.7 %copy-start.16 = (s32[64,1]{0,1:T(1,128)S(1)}, s32[64,1]{0,1:T(1,128)}, u32[]{:S(2)}) copy-start(s32[64,1]{0,1:T(1,128)} %param.31) | copy-start | bytes 772
  2.6 0.8 %copy-start.15 = (f32[4,56,21]{1,0,2:T(4,128)S(1)}, f32[4,56,21]{1,0,2:T(4,128)}, u32[]{:S(2)}) copy-start(f32[4,56,21]{1,0,2:T(4,128)} %param.24) | copy-start | bytes 56452
  3.4 0.9 %copy-start.10 = (f32[3,56,56]{2,1,0:T(8,128)S(1)}, f32[3,56,56]{2,1,0:T(8,128)}, u32[]{:S(2)}) copy-start(f32[3,56,56]{2,1,0:T(8,128)} %param.22) | copy-start | bytes 112900
  4.4 0.9 %copy-start.13 = (f32[3,9,9,128]{3,0,2,1:T(4,128)S(1)}, f32[3,9,9,128]{3,0,2,1:T(4,128)}, u32[]{:S(2)}) copy-start(f32[3,9,9,128]{3,0,2,1:T(4,128)} %param.19) | copy-start | bytes 373252
  5.3 0.9 %copy-start.11 = (f32[4,9,9,128]{3,0,2,1:T(4,128)S(1)}, f32[4,9,9,128]{3,0,2,1:T(4,128)}, u32[]{:S(2)}) copy-start(f32[4,9,9,128]{3,0,2,1:T(4,128)} %param.20) | copy-start | bytes 497668
  6.2 0.9 %copy-start.12 = (f32[4,9,9,128]{3,0,2,1:T(4,128)S(1)}, f32[4,9,9,128]{3,0,2,1:T(4,128)}, u32[]{:S(2)}) copy-start(f32[4,9,9,128]{3,0,2,1:T(4,128)} %param.21) | copy-start | bytes 497668
  7.2 0.9 %copy-start.1 = (f32[9,56,128]{2,1,0:T(8,128)S(1)}, f32[9,56,128]{2,1,0:T(8,128)}, u32[]{:S(2)}) copy-start(f32[9,56,128]{2,1,0:T(8,128)} %wave.1) | copy-start | bytes 774148
  7.2 0.9 %copy-start.2 = (s32[4,128]{1,0:T(4,128)S(1)}, s32[4,128]{1,0:T(4,128)}, u32[]{:S(2)}) copy-start(s32[4,128]{1,0:T(4,128)} %source.1) | copy-start | bytes 6148
  7.2 0.9 %copy-start.3 = (s32[128]{0:T(128)S(1)}, s32[128]{0:T(128)}, u32[]{:S(2)}) copy-start(s32[128]{0:T(128)} %param.25) | copy-start | bytes 1540
  7.2 0.9 %copy-start.4 = (f32[128]{0:T(128)S(1)}, f32[128]{0:T(128)}, u32[]{:S(2)}) copy-start(f32[128]{0:T(128)} %param.26) | copy-start | bytes 1540
  7.2 0.9 %copy-start.5 = (s32[128]{0:T(128)S(1)}, s32[128]{0:T(128)}, u32[]{:S(2)}) copy-start(s32[128]{0:T(128)} %param.27) | copy-start | bytes 1540
  7.2 0.9 %copy-start.6 = (s32[1,64]{1,0:T(1,128)S(1)}, s32[1,64]{1,0:T(1,128)}, u32[]{:S(2)}) copy-start(s32[1,64]{1,0:T(1,128)} %faults.1) | copy-start | bytes 772
  7.2 0.9 %copy-start.7 = (f32[128]{0:T(128)S(1)}, f32[128]{0:T(128)}, u32[]{:S(2)}) copy-start(f32[128]{0:T(128)} %param.32) | copy-start | bytes 1540
  7.2 0.9 %copy-start.8 = (f32[128]{0:T(128)S(1)}, f32[128]{0:T(128)}, u32[]{:S(2)}) copy-start(f32[128]{0:T(128)} %param.33) | copy-start | bytes 1540
  7.2 0.9 %copy-start.9 = (s32[128]{0:T(128)S(1)}, s32[128]{0:T(128)}, u32[]{:S(2)}) copy-start(s32[128]{0:T(128)} %param.34) | copy-start | bytes 1540
where the time goes:
time: 35.7 us; the launch traced here: 35.4 us
  Pallas kernels  26 us (73%)
  local copies, waits for them, and re-layouts  8.55 us (24%)
  between operations  0.83 us (2%)
    pallas_call x1, Pallas kernels, local(): pl.pallas_call(functools.partial(kernel, (nx, ny, points)), out_shape=(ja...  26 us
    unnamed x44, local copies, waits for them, and re-layouts  7.58 us

commit v1 on v0

--- a/solution.py
+++ b/solution.py
@@ -35,10 +35,12 @@
     return jnp.concatenate([x, low_part(x)], axis=0).astype(BF16)
 
 
-def dot_split(mat, data):
-    rows = mat.shape[0]
-    top = dot(two_parts(mat), data.astype(BF16))
-    return top[:rows] + (top[rows:] + dot(mat.astype(BF16), low_part(data).astype(BF16)))
+def left_parts(mat):
+    return jnp.concatenate([mat, low_part(mat), mat], axis=1).astype(BF16)
+
+
+def right_parts(data):
+    return jnp.concatenate([data, data, low_part(data)], axis=0).astype(BF16)
 
 
 def pick(parts, select):
@@ -49,14 +51,13 @@
 
 def kernel(
     cfg,
-    wave,
-    star,
-    own_mats,
-    nbr_mats,
-    stiff,
-    stiff_t,
-    proj,
-    lift,
+    wave_hbm,
+    star_hbm,
+    own_hbm,
+    nbr_hbm,
+    stiff_hbm,
+    proj_hbm,
+    lift_hbm,
     cluster,
     yield_stress,
     mask,
@@ -69,6 +70,13 @@
     flag,
     out,
     slip_out,
+    wave,
+    star,
+    own_mats,
+    nbr_mats,
+    stiff_in,
+    proj_in,
+    lift_in,
     deriv,
     early,
     late,
@@ -79,6 +87,11 @@
     own_tab,
     nbr_tab,
     flux,
+    faces_in,
+    stiff,
+    stiff_t,
+    proj,
+    lift,
     select,
     send_select,
     fault_select,
@@ -97,12 +110,13 @@
     ret_recv,
     tr_send,
     tr_recv,
+    in_sems,
 ):
     nx, ny, points = cfg
     modes, elems = wave.shape[1:]
     rows = up8(points)
     faces = 4 * elems
-    slot_count = sends.shape[1] // 4
+    slot_count = sends.shape[1]
     group = packs.shape[2]
     table_rows = VARS * rows
     cap = slip0.shape[1] // ny
@@ -120,20 +134,35 @@
     for target in [x_up, x_down] + [peer(t) for t in range(1, ny)]:
         pl.semaphore_signal(barrier, inc=1, device_id=target, device_id_type=MESH)
 
+    fetches = {}
+    for k, (src, dst) in enumerate(
+        (
+            (stiff_hbm, stiff_in),
+            (proj_hbm, proj_in),
+            (lift_hbm, lift_in),
+            (wave_hbm, wave),
+            (star_hbm, star),
+            (own_hbm, own_mats),
+            (nbr_hbm, nbr_mats),
+        )
+    ):
+        fetches[k] = pltpu.make_async_copy(src, dst, in_sems.at[k])
+        fetches[k].start()
     me = iy.astype(F32)
     table_size = select.shape[0]
     for f in range(4):
         want = source[f : f + 1, :].astype(F32)
         hit = iota_f((table_size, elems), 0) == want
         select[:, f * elems : (f + 1) * elems] = jnp.where(hit, 1.0, 0.0).astype(BF16)
-    hit = iota_f((faces, 4 * slot_count), 0) == sends[...].astype(F32)
+    row = jnp.concatenate([sends[d : d + 1, :] for d in (1, 0, 3, 2)], axis=1)
+    hit = iota_f((faces, 4 * slot_count), 0) == row.astype(F32)
     send_select[...] = jnp.where(hit, 1.0, 0.0).astype(BF16)
     count = faults.shape[1]
     hit = iota_f((faces, count), 0) == faults[...].astype(F32)
     fault_select[...] = jnp.where(hit, 1.0, 0.0)
-    owner_col = owners[...].astype(F32)
+    owner_row = owners[...].astype(F32)
     r, c = iota_f((count, count), 0), iota_f((count, count), 1)
-    owner_row = jnp.sum(jnp.where(r == c, owner_col, 0.0), axis=0, keepdims=True)
+    owner_col = jnp.sum(jnp.where(r == c, owner_row, 0.0), axis=1, keepdims=True)
     same = jnp.where((owner_col == owner_row) & (r < c), 1.0, 0.0)
     rank = jnp.sum(same, axis=0, keepdims=True)
     slot_row = me * cap + rank
@@ -142,21 +171,41 @@
     ahead = jnp.where(away < 0, away + ny, away)
     behind = jnp.where(away > 0, ny - away, -away)
 
-    def mix_all(src, field):
-        def one_dir(d, carry):
-            at = pl.ds(pl.multiple_of(d * modes, 8), modes)
-            for first in range(0, VARS, 3):
-                accs = [None] * 3
-                for s in range(VARS):
-                    value = field[s]
-                    for k in range(3):
-                        term = star[d, first + k, s : s + 1, :] * value
-                        accs[k] = term if s == 0 else accs[k] + term
+    for k in range(3):
+        fetches[k].wait()
+    stiff[...] = left_parts(stiff_in[...].reshape(3 * modes, modes))
+    turned = [jnp.transpose(stiff_in[d]) for d in range(3)]
+    stiff_t[...] = left_parts(jnp.concatenate(turned, axis=0))
+    for source_in, kept in ((proj_in, proj), (lift_in, lift)):
+        faces_in[...] = jnp.zeros_like(faces_in)
+        for f in range(4):
+            faces_in[f * rows : f * rows + points, :] = source_in[:, f, :]
+        if kept is proj:
+            kept[...] = left_parts(faces_in[...])
+        else:
+            kept[...] = left_parts(jnp.transpose(faces_in[...]))
+
+    def flat(field):
+        return right_parts(jnp.concatenate([field[v] for v in range(VARS)], axis=1))
+
+    def star_sum(first):
+        accs = [None] * 3
+        for d in range(3):
+            for s in range(VARS):
+                value = mix[d * modes : (d + 1) * modes, s * elems : (s + 1) * elems]
                 for k in range(3):
-                    mix[at, (first + k) * elems : (first + k + 1) * elems] = accs[k]
-            return carry
-
-        lax.fori_loop(0, 3, one_dir, 0)
+                    term = star[first + k, s, d : d + 1, :] * value
+                    accs[k] = term if accs[k] is None else accs[k] + term
+        return accs
+
+    def face_sum(mats, table, first, f):
+        accs = [None] * 3
+        for s in range(VARS):
+            value = table[s * rows : (s + 1) * rows, f * elems : (f + 1) * elems]
+            for k in range(3):
+                term = mats[first + k, s, f : f + 1, :] * value
+                accs[k] = term if s == 0 else accs[k] + term
+        return accs
 
     def predict(src, with_late):
         for v in range(VARS):
@@ -173,21 +222,26 @@
                 scale_late = jnp.where(
                     power == p, (2.0**p - 1.0) / math.factorial(p), scale_late
                 )
-            mix_all(None, deriv)
-            change = dot_split(stiff[...], mix[...])
-            for v in range(VARS):
-                step = -change[:, v * elems : (v + 1) * elems]
-                deriv[v] = step
-                early[v] += step * scale_early
-                if with_late:
-                    late[v] += step * scale_late
-            return carry
+            mix[...] = dot(stiff[...], flat(deriv))
+
+            def some_vars(third, inner):
+                accs = star_sum(third * 3)
+                for k in range(3):
+                    v = third * 3 + k
+                    step = -accs[k]
+                    deriv[v] = step
+                    early[v] += step * scale_early
+                    if with_late:
+                        late[v] += step * scale_late
+                return inner
+
+            return lax.fori_loop(0, 3, some_vars, carry)
 
         lax.fori_loop(2, ORDER + 1, one_power, 0)
 
     def advance(field, turn):
-        flat = jnp.concatenate([field[v] for v in range(VARS)], axis=1)
-        traces = dot_split(proj[...], flat)
+        held = flat(field)
+        traces = dot(proj[...], held)
         for v in range(VARS):
             for f in range(4):
                 own_tab[v * rows : (v + 1) * rows, f * elems : (f + 1) * elems] = traces[
@@ -218,26 +272,25 @@
             copy.start()
             copies.append(copy)
 
-        mix_all(None, field)
-        volume = dot_split(stiff_t[...], mix[...])
-        for v in range(VARS):
-            inc[v] = volume[:, v * elems : (v + 1) * elems]
+        mix[...] = dot(stiff_t[...], held)
         nbr_tab[...] = pick(own_parts, select[0:faces, :])
 
-        def own_flux(f, carry):
-            lanes = pl.ds(pl.multiple_of(f * elems, elems), elems)
-            at = pl.ds(pl.multiple_of(f * rows, 8), rows)
-            accs = [None] * VARS
-            for s in range(VARS):
-                value = own_tab[s * rows : (s + 1) * rows, lanes]
-                for i in range(VARS):
-                    term = own_mats[f, i, s : s + 1, :] * value
-                    accs[i] = term if s == 0 else accs[i] + term
-            for i in range(VARS):
-                flux[at, i * elems : (i + 1) * elems] = accs[i]
+        def own_side(third, carry):
+            first = third * 3
+            accs = star_sum(first)
+            for k in range(3):
+                inc[first + k] = accs[k]
+            for f in range(4):
+                accs = face_sum(own_mats, own_tab, first, f)
+                for k in range(3):
+                    lanes = pl.ds(pl.multiple_of((first + k) * elems, elems), elems)
+                    flux[f * rows : (f + 1) * rows, lanes] = accs[k]
             return carry
 
-        lax.fori_loop(0, 4, own_flux, 0)
+        if turn == 0:
+            fetches[5].wait()
+            fetches[6].wait()
+        lax.fori_loop(0, 3, own_side, 0)
         if turn == 0:
             for copy in par_copies:
                 copy.wait_recv()
@@ -271,15 +324,20 @@
             table_in[g * group : (g + 1) * group, :] = total
         nbr_tab[...] += pick(two_parts(table_in[0:table_rows, :]), select[faces:, :])
 
-        def face_flux(f, carry):
+        def nbr_side(third, carry):
+            first = third * 3
+            for f in range(4):
+                accs = face_sum(nbr_mats, nbr_tab, first, f)
+                for k in range(3):
+                    lanes = pl.ds(pl.multiple_of((first + k) * elems, elems), elems)
+                    flux[f * rows : (f + 1) * rows, lanes] += accs[k]
+            return carry
+
+        lax.fori_loop(0, 3, nbr_side, 0)
+
+        def fault_flux(f, carry):
             lanes = pl.ds(pl.multiple_of(f * elems, elems), elems)
             at = pl.ds(pl.multiple_of(f * rows, 8), rows)
-            accs = [None] * VARS
-            for s in range(VARS):
-                value = nbr_tab[s * rows : (s + 1) * rows, lanes]
-                for i in range(VARS):
-                    term = nbr_mats[f, i, s : s + 1, :] * value
-                    accs[i] = term if s == 0 else accs[i] + term
             state = []
             for tv, vv in ((0, 6), (3, 7), (5, 8)):
                 m_t = own_tab[tv * rows : (tv + 1) * rows, lanes]
@@ -293,16 +351,14 @@
             size = jnp.sqrt(state[1] * state[1] + state[2] * state[2])
             slipping = face_par[2:3, lanes] > 0.5
             ratio = jnp.where(slipping, strength / jnp.maximum(size, strength), 1.0)
-            accs[3] = accs[3] + state[1] * (ratio - 1.0)
-            accs[5] = accs[5] + state[2] * (ratio - 1.0)
-            for i in range(VARS):
-                flux[at, i * elems : (i + 1) * elems] += accs[i]
+            flux[at, 3 * elems : 4 * elems] += state[1] * (ratio - 1.0)
+            flux[at, 5 * elems : 6 * elems] += state[2] * (ratio - 1.0)
             gain = jnp.sum(size * (1.0 - ratio), axis=0, keepdims=True) / points
             face_par[0:1, lanes] = slip + gain
             moved[0:1, lanes] += gain
             return carry
 
-        lax.fori_loop(0, 4, face_flux, 0)
+        lax.fori_loop(0, 4, fault_flux, 0)
         if turn == 1:
             per_fault = jnp.dot(
                 moved[...], fault_select[...], precision=HIGHEST, preferred_element_type=F32
@@ -329,7 +385,7 @@
                 )
                 copy.start()
                 ret_copies.append(copy)
-        lifted = dot_split(lift[...], flux[...])
+        lifted = dot(lift[...], right_parts(flux[...]))
         for v in range(VARS):
             inc[v] -= lifted[:, v * elems : (v + 1) * elems]
         trace_copies.extend(copies)
@@ -347,6 +403,8 @@
         return [mean + factor * d for d in dev] + [factor * values[v] for v in range(3, 6)]
 
     par_copies, ret_copies, trace_copies = [], [], []
+    fetches[3].wait()
+    fetches[4].wait()
     predict(wave, True)
     pl.semaphore_wait(barrier, ny + 1)
     par[0] = jnp.zeros(par.shape[1:], F32)
@@ -414,14 +472,16 @@
     slot_count = send_faces.shape[1]
     count = fault_faces.shape[1]
     owned = fault_slip.shape[0]
-    pad = rows - points
-    stiff = jnp.transpose(stiffness, (1, 0, 2)).reshape(modes, 3 * modes)
-    stiff_t = jnp.transpose(stiffness, (2, 0, 1)).reshape(modes, 3 * modes)
-    proj = jnp.pad(face_proj, ((0, 0), (0, pad), (0, 0))).reshape(4 * rows, modes)
-    lift = jnp.pad(jnp.transpose(lift_mats, (1, 0, 2)), ((0, 0), (0, 0), (0, pad)))
-    lift = lift.reshape(modes, 4 * rows)
-    sends = send_faces[jnp.array([1, 0, 3, 2])].reshape(1, 4 * slot_count)
     group = up8(-(-VARS * rows // 4))
+    fetched = (
+        wavefield,
+        jnp.transpose(star_mats, (1, 2, 0, 3)),
+        jnp.transpose(flux_own, (1, 2, 0, 3)),
+        jnp.transpose(flux_nbr, (1, 2, 0, 3)),
+        stiffness,
+        jnp.transpose(face_proj, (1, 0, 2)),
+        jnp.transpose(lift_mats, (2, 0, 1)),
+    )
     field = pltpu.VMEM((VARS, modes, elems), F32)
     vmem = pl.BlockSpec(memory_space=pltpu.VMEM)
     out, slip = pl.pallas_call(
@@ -430,14 +490,20 @@
             jax.ShapeDtypeStruct(wavefield.shape, F32),
             jax.ShapeDtypeStruct((1, owned), F32),
         ),
-        in_specs=[vmem] * 18,
+        in_specs=[pl.BlockSpec(memory_space=pl.ANY)] * 7 + [vmem] * 10,
         out_specs=(vmem, vmem),
-        scratch_shapes=[field] * 6
+        scratch_shapes=[pltpu.VMEM(x.shape, F32) for x in fetched]
+        + [field] * 6
         + [
             pltpu.VMEM((3 * modes, VARS * elems), F32),
             pltpu.VMEM((VARS * rows, 4 * elems), F32),
             pltpu.VMEM((VARS * rows, 4 * elems), F32),
             pltpu.VMEM((4 * rows, VARS * elems), F32),
+            pltpu.VMEM((4 * rows, modes), F32),
+            pltpu.VMEM((3 * modes, 3 * modes), BF16),
+            pltpu.VMEM((3 * modes, 3 * modes), BF16),
+            pltpu.VMEM((4 * rows, 3 * modes), BF16),
+            pltpu.VMEM((modes, 12 * rows), BF16),
             pltpu.VMEM((4 * elems + 4 * slot_count, 4 * elems), BF16),
             pltpu.VMEM((4 * elems, 4 * slot_count), BF16),
             pltpu.VMEM((4 * elems, count), F32),
@@ -456,26 +522,20 @@
             pltpu.SemaphoreType.DMA((ny,)),
             pltpu.SemaphoreType.DMA((2, 4)),
             pltpu.SemaphoreType.DMA((2, 4)),
+            pltpu.SemaphoreType.DMA((len(fetched),)),
         ],
         compiler_params=pltpu.CompilerParams(
-            collective_id=0, has_side_effects=True, vmem_limit_bytes=48 * 1024 * 1024
+            collective_id=0, has_side_effects=True, vmem_limit_bytes=60 * 1024 * 1024
         ),
     )(
-        wavefield,
-        star_mats,
-        flux_own,
-        flux_nbr,
-        stiff,
-        stiff_t,
-        proj,
-        lift,
+        *fetched,
         cluster.reshape(1, elems),
         yield_stress.reshape(1, elems),
         plastic_mask.reshape(1, elems),
         face_source,
-        sends,
+        send_faces,
         fault_faces,
-        fault_owner,
+        fault_owner.reshape(1, count),
         fault_slip.reshape(1, owned),
         cohesion.reshape(1, owned),
         slip_flag.reshape(1, owned),

time: 35.7 us -> 32.4 us (0.908)
  local copies, waits for them, and re-layouts: 8.55 us -> 2.18 us
  Pallas kernels: 26 us -> 29.4 us
    unnamed x44 -> x4, local copies, waits for them, and re-layouts: 7.58 us -> 2.18 us
    pallas_call x1, Pallas kernels: 26 us -> 29.4 us  [local(): pl.pallas_call(functools.partial(kernel, (nx, ny, points)), out_shape=(ja...]
    gather x1 -> x0, local copies, waits for them, and re-layouts: 0.56 us -> none  [local(): sends = send_faces[jnp.array([1, 0, 3, 2])].reshape(1, 4 * slot_count)]
where the time goes in v1:
time: 32.4 us; the launch traced here: 32.2 us
  Pallas kernels  29.4 us (91%)
  local copies, waits for them, and re-layouts  2.18 us (7%)
  between operations  0.65 us (2%)
    pallas_call x1, Pallas kernels, local(): pl.pallas_call(functools.partial(kernel, (nx, ny, points)), out_shape=(ja...  29.4 us
    unnamed x4, local copies, waits for them, and re-layouts  2.18 us

profile of v1, /device:TPU:0, one launch (start us, length us, event | category | flops | bytes accessed | tf_op | source)
XLA Modules:
  0.0 32.2 jit_solution(13160220268706796712)
XLA Ops:
  0.6 29.4 %shard_map.176 = (f32[9,56,128]{2,1,0:T(8,128)}, f32[1,128]{1,0:T(1,128)}) custom-call(f32[9,56,128]{2,1,0:T(8,128)} %wave_hbm.1, f32[9,9,3,128]{3,2,1,0:T(4,128)} %bitcast.13, f32[9,9,4,128]{3,2,1,0:T(4,128)} %bitcast.14, f32[9,9,4,128]{3,2,1,0:T(4,128)} %bitcast.15, f32[3,56,56]{2,1,0:T(8,128)} %stiff_hbm.1, f32[21,4,56]{2,1,0:T(4,128)} %bitcast.16, ...), custom_call_target="tpu_custom_call" | custom-call | tf_op jit(solution)/shard_map/pallas_call | solution.py:487
  30.1 0.0 copy-start
  30.1 1.7 %copy.21 = f32[9,56,128]{2,1,0:T(8,128)} copy(f32[9,56,128]{2,1,0:T(8,128)} %get-tuple-element.8) | data formatting | bytes 516096
  31.7 0.0 copy-done
  31.7 0.5 %copy.22 = f32[128]{0:T(128)} copy(f32[128]{0:T(128)S(1)} %bitcast.25) | data formatting | bytes 1024
Async XLA Ops:
  30.1 1.7 %copy-start = (f32[1,128]{1,0:T(1,128)S(1)}, f32[1,128]{1,0:T(1,128)}, u32[]{:S(2)}) copy-start(f32[1,128]{1,0:T(1,128)} %get-tuple-element.5) | copy-start | bytes 1540

commit v2 on v1

--- a/solution.py
+++ b/solution.py
@@ -149,11 +149,6 @@
         fetches[k] = pltpu.make_async_copy(src, dst, in_sems.at[k])
         fetches[k].start()
     me = iy.astype(F32)
-    table_size = select.shape[0]
-    for f in range(4):
-        want = source[f : f + 1, :].astype(F32)
-        hit = iota_f((table_size, elems), 0) == want
-        select[:, f * elems : (f + 1) * elems] = jnp.where(hit, 1.0, 0.0).astype(BF16)
     row = jnp.concatenate([sends[d : d + 1, :] for d in (1, 0, 3, 2)], axis=1)
     hit = iota_f((faces, 4 * slot_count), 0) == row.astype(F32)
     send_select[...] = jnp.where(hit, 1.0, 0.0).astype(BF16)
@@ -272,6 +267,12 @@
             copy.start()
             copies.append(copy)
 
+        if turn == 0:
+            table_size = select.shape[0]
+            for f in range(4):
+                want = source[f : f + 1, :].astype(F32)
+                hit = iota_f((table_size, elems), 0) == want
+                select[:, f * elems : (f + 1) * elems] = jnp.where(hit, 1.0, 0.0).astype(BF16)
         mix[...] = dot(stiff_t[...], held)
         nbr_tab[...] = pick(own_parts, select[0:faces, :])
 

time: 32.4 us -> 32.4 us (level)
  no operation moved by 1% of the time
where the time goes in v2:
time: 32.4 us; the launch traced here: 32.2 us
  Pallas kernels  29.4 us (91%)
  local copies, waits for them, and re-layouts  2.18 us (7%)
  between operations  0.65 us (2%)
    pallas_call x1, Pallas kernels, local(): pl.pallas_call(functools.partial(kernel, (nx, ny, points)), out_shape=(ja...  29.4 us
    unnamed x4, local copies, waits for them, and re-layouts  2.18 us

profile of v2, /device:TPU:0, one launch (start us, length us, event | category | flops | bytes accessed | tf_op | source)
XLA Modules:
  0.0 32.2 jit_solution(9350858307710409148)
XLA Ops:
  0.6 29.4 %shard_map.176 = (f32[9,56,128]{2,1,0:T(8,128)}, f32[1,128]{1,0:T(1,128)}) custom-call(f32[9,56,128]{2,1,0:T(8,128)} %wave_hbm.1, f32[9,9,3,128]{3,2,1,0:T(4,128)} %bitcast.13, f32[9,9,4,128]{3,2,1,0:T(4,128)} %bitcast.14, f32[9,9,4,128]{3,2,1,0:T(4,128)} %bitcast.15, f32[3,56,56]{2,1,0:T(8,128)} %stiff_hbm.1, f32[21,4,56]{2,1,0:T(4,128)} %bitcast.16, ...), custom_call_target="tpu_custom_call" | custom-call | tf_op jit(solution)/shard_map/pallas_call | solution.py:488
  30.1 0.0 copy-start
  30.1 1.7 %copy.21 = f32[9,56,128]{2,1,0:T(8,128)} copy(f32[9,56,128]{2,1,0:T(8,128)} %get-tuple-element.8) | data formatting | bytes 516096
  31.7 0.0 copy-done
  31.7 0.5 %copy.22 = f32[128]{0:T(128)} copy(f32[128]{0:T(128)S(1)} %bitcast.25) | data formatting | bytes 1024
Async XLA Ops:
  30.1 1.7 %copy-start = (f32[1,128]{1,0:T(1,128)S(1)}, f32[1,128]{1,0:T(1,128)}, u32[]{:S(2)}) copy-start(f32[1,128]{1,0:T(1,128)} %get-tuple-element.5) | copy-start | bytes 1540
